TPU v7x, 256 devices: a whole 4x4x8 slice. The times are simulated.
256 devices in a mesh: dp: 8 (over y, x_lo), seq: 32 (over z, x_hi, core).
Axes of the slice: x: 4 (x_hi: 2, x_lo: 2; x = x_hi * 2 + x_lo), y: 4, z: 8, core: 2. Of those that a mesh axis runs over, the one named last changes fastest.
Arguments:
- context_ids: int32 [262144], P(('dp', 'seq')), parts along dimension 0, may hold values from 0 to 255
- embed_table: bfloat16 [256, 1024], replicated, may hold values from -6 to 6
- latent_states: bfloat16 [2048, 1024], P(('dp', 'seq')), parts along dimension 0, may hold values from -3 to 3
- limits: int32 [2048], P('dp'), parts along dimension 0, may hold values from 16385 to 32768, as said below
- cross_q: bfloat16 [1024, 1024], replicated
- cross_kv: bfloat16 [1024, 2048], replicated, may hold values from -0.1875 to 0.1875
- cross_o: bfloat16 [1024, 1024], replicated, may hold values from -0.75 to 0.75
- attn_gain: float32 [1024], replicated, may hold values from 0.1 to 1.9
- self_qkv: bfloat16 [1024, 3072], P(None, 'seq')
- self_o: bfloat16 [1024, 1024], P(None, 'seq'), may hold values from -0.1875 to 0.1875
- mlp_gain: float32 [1024], replicated, may hold values from 0.1 to 1.9
- mlp_up: bfloat16 [1024, 4096], P(None, 'seq'), may hold values from -0.1875 to 0.1875
- mlp_down: bfloat16 [4096, 1024], P('seq'), may hold values from -0.1875 to 0.1875
Outputs:
- updated_latents: float32 [2048, 1024], P(('dp', 'seq')), parts along dimension 0
There are 8 independent parts, one for each index of `dp`. A program takes and returns all parts, laid end to end along the dimension named above; an argument that names none is the same for every part. Nothing has to cross between parts.
Inputs may be any that keep to these rules, and one draw needn't show every extreme that they name: `limits`: non-decreasing along the latent rows; the first row sees 32768 // 2 + 1 positions and the last row all 32768.
All inputs are finite; a program needn't handle non-finite values.
Results may differ from a plain program's by a relative error of at most 0.02.
The roundings to bfloat16 on the way count: a program that leaves them out, or rounds other values in their place, can miss the bound.
Values may be sent and summed in bfloat16 or wider, within the bound.
A program may use at most 128 MiB of HBM per device.

v0:
```python
import math

import jax
import jax.numpy as jnp
from jax import lax
from jax.sharding import PartitionSpec as P

HEADS = 16


def rms_scale(states, gain):
    mean_sq = jnp.mean(states * states, axis=-1, keepdims=True)
    return states * lax.rsqrt(mean_sq + 1e-05) * gain


def rotate_rows(rows_in, positions, head_size):
    half_size = head_size // 2
    period_list = [
        int(4.0 * 16384.0 ** (freq_index / (half_size - 1))) for freq_index in range(half_size)
    ]
    periods = jnp.array(period_list, dtype=jnp.int32)
    factors = jnp.array([2.0 * math.pi / period for period in period_list], dtype=jnp.float32)
    phase = (positions[:, None] % periods[None, :]).astype(jnp.float32) * factors[None, :]
    cosines = jnp.cos(phase)[:, None, :]
    sine_values = jnp.sin(phase)[:, None, :]
    count_rows = rows_in.shape[0]
    parted = rows_in.reshape(count_rows, -1, head_size)
    first_half = parted[..., :half_size]
    second_half = parted[..., half_size:]
    turned = jnp.concatenate(
        [
            first_half * cosines - second_half * sine_values,
            second_half * cosines + first_half * sine_values,
        ],
        axis=-1,
    )
    return turned.reshape(count_rows, -1).astype(jnp.bfloat16)


def on_device(
    context_ids,
    embed_table,
    latent_states,
    limits,
    cross_q,
    cross_kv,
    cross_o,
    attn_gain,
    self_qkv,
    self_o,
    mlp_gain,
    mlp_up,
    mlp_down,
):
    seq_count = lax.axis_size("seq")
    seq_rank = lax.axis_index("seq")
    ctx_rows = context_ids.shape[0]
    lat_rows = latent_states.shape[0]
    model_width = embed_table.shape[1]
    head_count = HEADS
    head_size = model_width // head_count
    total_lat = lat_rows * seq_count
    score_scale = 1.0 / math.sqrt(head_size)
    positions = seq_rank * ctx_rows + jnp.arange(ctx_rows, dtype=jnp.int32)
    onehot = (
        context_ids[:, None] == jnp.arange(embed_table.shape[0], dtype=jnp.int32)[None, :]
    ).astype(jnp.bfloat16)
    embedded = jnp.dot(onehot, embed_table, preferred_element_type=jnp.float32).astype(jnp.bfloat16)
    key_value = jnp.dot(embedded, cross_kv, preferred_element_type=jnp.float32)
    context_keys = rotate_rows(key_value[:, :model_width], positions, head_size).reshape(
        ctx_rows, head_count, head_size
    )
    context_values = (
        key_value[:, model_width:].astype(jnp.bfloat16).reshape(ctx_rows, head_count, head_size)
    )
    states_all = lax.all_gather(latent_states, "seq", axis=0, tiled=True)
    raw_queries = jnp.dot(states_all, cross_q, preferred_element_type=jnp.float32)
    queries = rotate_rows(raw_queries, limits - 1, head_size)
    block_rows = min(512, total_lat)
    block_count = total_lat // block_rows
    query_blocks = queries.reshape(block_count, block_rows, head_count, head_size)
    limit_blocks = limits.reshape(block_count, block_rows)

    def cross_block(state_in, inputs):
        query_part, limit_part = inputs
        scores = (
            jnp.einsum("qhd,khd->hqk", query_part, context_keys, preferred_element_type=jnp.float32)
            * score_scale
        )
        visible = (positions[None, :] < limit_part[:, None])[None]
        masked = jnp.where(visible, scores, -1e30)
        row_peak = jnp.max(masked, axis=2)
        weights = jnp.where(visible, jnp.exp(masked - row_peak[:, :, None]), 0.0).astype(
            jnp.bfloat16
        )
        row_total = jnp.sum(weights, axis=2, dtype=jnp.float32)
        numerators = jnp.einsum(
            "hqk,khd->qhd", weights, context_values, preferred_element_type=jnp.float32
        )
        return (state_in, (numerators.reshape(block_rows, model_width), row_peak.T, row_total.T))

    _, (numerators, block_peak, block_total) = lax.scan(
        cross_block, 0, (query_blocks, limit_blocks)
    )
    numerators = numerators.reshape(total_lat, model_width)
    block_peak = block_peak.reshape(total_lat, head_count)
    block_total = block_total.reshape(total_lat, head_count)
    row_top = lax.pmax(block_peak, "seq")
    rescale = jnp.exp(block_peak - row_top)
    scaled = (numerators.reshape(total_lat, head_count, head_size) * rescale[..., None]).reshape(
        total_lat, model_width
    )
    owned_flat, owned_total = (
        lax.psum_scatter(scaled, "seq", scatter_dimension=0, tiled=True),
        lax.psum_scatter(block_total * rescale, "seq", scatter_dimension=0, tiled=True),
    )
    owned_numer = owned_flat.reshape(lat_rows, head_count, head_size)
    cross_mix = (
        (owned_numer / owned_total[..., None]).reshape(lat_rows, model_width).astype(jnp.bfloat16)
    )
    latents = latent_states.astype(jnp.float32) + jnp.dot(
        cross_mix, cross_o, preferred_element_type=jnp.float32
    )
    normed = rms_scale(latents, attn_gain).astype(jnp.bfloat16)
    column_part = jnp.dot(
        lax.all_gather(normed, "seq", axis=0, tiled=True),
        self_qkv,
        preferred_element_type=jnp.float32,
    ).astype(jnp.bfloat16)
    projected = lax.all_to_all(column_part, "seq", split_axis=0, concat_axis=1, tiled=True)
    self_queries = projected[:, :model_width].reshape(lat_rows, head_count, head_size)
    owned_key_value = projected[:, model_width:]
    my_pos = seq_rank * lat_rows + jnp.arange(lat_rows, dtype=jnp.int32)
    shard_rows = lax.all_gather(owned_key_value, "seq", axis=0, tiled=True)
    running_peak = jnp.full((head_count, lat_rows), -1e30, jnp.float32)
    count_rows = shard_rows.shape[0]
    remote_keys = shard_rows[:, :model_width].reshape(count_rows, head_count, head_size)
    remote_values = (
        shard_rows[:, model_width:].reshape(count_rows, head_count, head_size).astype(jnp.float32)
    )
    scores = (
        jnp.einsum("qhd,khd->hqk", self_queries, remote_keys, preferred_element_type=jnp.float32)
        * score_scale
    )
    key_pos = jnp.arange(count_rows, dtype=jnp.int32)
    visible = (key_pos[None, :] <= my_pos[:, None])[None]
    masked = jnp.where(visible, scores, -1e30)
    new_peak = jnp.maximum(running_peak, jnp.max(masked, axis=2))
    weights = jnp.where(visible, jnp.exp(masked - new_peak[:, :, None]), 0.0)
    new_total = jnp.sum(weights, axis=2)
    product = jnp.einsum("hqk,khd->hqd", weights, remote_values, precision=lax.Precision.HIGHEST)
    mixed = product / new_total[..., None]
    self_mix = jnp.transpose(mixed, (1, 0, 2)).reshape(lat_rows, model_width).astype(jnp.bfloat16)
    out_part = jnp.dot(
        lax.all_gather(self_mix, "seq", axis=0, tiled=True),
        self_o,
        preferred_element_type=jnp.float32,
    )
    attended = latents + lax.all_to_all(
        out_part.astype(jnp.bfloat16), "seq", split_axis=0, concat_axis=1, tiled=True
    ).astype(out_part.dtype)
    normed_mlp = rms_scale(attended, mlp_gain).astype(jnp.bfloat16)
    hidden = jax.nn.gelu(
        jnp.dot(
            lax.all_gather(normed_mlp, "seq", axis=0, tiled=True),
            mlp_up,
            preferred_element_type=jnp.float32,
        ),
        approximate=True,
    ).astype(jnp.bfloat16)
    mlp_terms = jnp.dot(hidden, mlp_down, preferred_element_type=jnp.float32)
    owned_sum = lax.psum_scatter(
        mlp_terms.astype(jnp.bfloat16), "seq", scatter_dimension=0, tiled=True
    ).astype(jnp.float32)
    return attended + owned_sum


def solution(mesh):
    placed = (
        P(("dp", "seq")),
        P(),
        P(("dp", "seq"), None),
        P("dp"),
        P(),
        P(),
        P(),
        P(),
        P(None, "seq"),
        P(None, "seq"),
        P(),
        P(None, "seq"),
        P("seq", None),
    )
    return jax.shard_map(
        on_device, mesh=mesh, in_specs=placed, out_specs=P(("dp", "seq"), None), check_vma=False
    )
```

profile of v0, /device:TPU:16, one launch (start us, length us, event | category | flops | bytes accessed | tf_op | source)
XLA Modules:
  0.0 715.4 jit_solution(1201293240516671348)
XLA Ops:
  6.5 10.8 %fusion.5 = f32[1024,2048]{1,0:T(8,128)} fusion(bf16[1024,2048]{1,0:T(8,128)(2,1)} %param.22, bf16[256,1024]{1,0:T(8,128)(2,1)} %param.18, s32[1024]{0:T(1024)} %param.17), kind=kOutput, calls=%fused_computation.11 | convolution fusion | flops 4833148928 | bytes 13111296 | tf_op jit(solution)/shard_map/dot_general | solution.py:69
  17.4 3.8 slice.60
  21.2 4.7 slice.44
  25.9 4.0 copy.35
  29.9 0.2 broadcast_compare_fusion
  30.2 5.4 copy.37
  35.5 46.4 %all_gather.15 = bf16[256,1024]{1,0:T(8,128)(2,1)S(1)} all-gather(bf16[8,1024]{1,0:T(8,128)(2,1)S(1)} %copy-done.5), channel_id=1, replica_groups=mesh['dp'=8,'seq'=32] {'seq'}, dimensions={0}, use_global_device_ids=true | all-gather | bytes 540672 | tf_op jit(solution)/shard_map/all_gather | solution.py:76
  81.9 1.8 fusion.30
  83.8 0.5 fusion.44
  84.3 1.0 fusion.57
  85.3 0.7 subtract_convert_fusion
  86.0 0.2 subtract_convert_fusion.1
  86.2 3.1 fusion
  89.3 5.2 convert_reduce_fusion
  94.4 0.6 copy-done.1
  95.0 128.8 %pmax.7 = f32[256,16]{0,1:T(8,128)S(1)} all-reduce(f32[256,16]{0,1:T(8,128)S(1)} %bitcast.60), channel_id=1, replica_groups=mesh['dp'=8,'seq'=32] {'seq'}, use_global_device_ids=true, to_apply=%region_1.2 | all-reduce | flops 4096 | bytes 32768 | tf_op jit(solution)/shard_map/pmax | solution.py:108
  223.8 8.7 %fusion.9 = f32[256,16,64]{0,2,1:T(8,128)S(1)} fusion(bf16[1024,16,64]{0,2,1:T(8,128)(2,1)} %bitcast.53, f32[256,16]{0,1:T(8,128)S(1)} %get-tuple-element.24, f32[16,256,1024]{2,1,0:T(8,128)} %copy-done.1, f32[16,256]{1,0:T(8,128)S(1)} %get-tuple-element.46, pred[256,1024]{1,0:T(8,128)(4,1)S(1)} %broadcast_compare_fusion), kind=kOutput, calls=%fused_computation.15 | convolution fusion | flops 558104576 | bytes 20217856 | tf_op jit(solution)/shard_map/while/body/eval_jaxpr/hqk,khd->qhd/dot_general | solution.py:97
  232.5 1.3 copy.47
  233.9 0.6 dynamic-slice.1
  235.1 128.9 %all-reduce = f32[256,16]{0,1:T(8,128)S(1)} all-reduce(f32[256,16]{0,1:T(8,128)S(1)} %get-tuple-element.23), channel_id=3, replica_groups=mesh['dp'=8,'seq'=32] {'seq'}, use_global_device_ids=true, to_apply=%region_4.5.clone | all-reduce | flops 4096 | bytes 32768
  364.1 1.0 copy.48
  365.1 2.1 multiply_reduce_fusion.1
  367.3 37.9 %all_gather.16 = bf16[256,1024]{1,0:T(8,128)(2,1)S(1)} all-gather(bf16[8,1024]{1,0:T(8,128)(2,1)S(1)} %multiply_convert_fusion.1), channel_id=1, replica_groups=mesh['dp'=8,'seq'=32] {'seq'}, dimensions={0}, use_global_device_ids=true | all-gather | bytes 540672 | tf_op jit(solution)/shard_map/all_gather | solution.py:126
  405.2 1.2 convolution_convert_fusion.1
  406.5 0.1 copy.38
  406.6 16.4 %all_to_all.32 = bf16[32,8,96]{2,1,0:T(8,128)(2,1)S(1)} all-to-all(bf16[32,8,96]{2,1,0:T(8,128)(2,1)S(1)} %bitcast.58), channel_id=1, replica_groups=mesh['dp'=8,'seq'=32] {'seq'}, dimensions={0} | all-to-all | bytes 98304 | tf_op jit(solution)/shard_map/all_to_all | solution.py:130
  423.0 0.1 all_to_all.27
  423.2 0.6 slice.48
  424.0 0.1 reshape.366
  424.1 72.6 %all-gather.2.cloned.1.call-done = bf16[256,2048]{1,0:T(8,128)(2,1)} async-done(((bf16[8,2048]{1,0:T(8,128)(2,1)}), bf16[256,2048]{1,0:T(8,128)(2,1)}) %all-gather.2.cloned.1.call-update) | async-done | bytes 1048592 | tf_op jit(solution)/shard_map/all_gather | solution.py:134
  496.7 1.3 fusion.53
  498.0 1.0 copy.42
  499.0 0.2 copy.40
  499.2 0.3 fusion.54
  499.5 0.2 fusion.32
  499.7 1.6 fusion.12
  501.3 0.1 convert_element_type.90
  501.4 39.9 %all_gather.18 = bf16[256,1024]{1,0:T(8,128)(2,1)S(1)} all-gather(bf16[8,1024]{1,0:T(8,128)(2,1)S(1)} %convert_element_type.90), channel_id=1, replica_groups=mesh['dp'=8,'seq'=32] {'seq'}, dimensions={0}, use_global_device_ids=true | all-gather | bytes 540672 | tf_op jit(solution)/shard_map/all_gather | solution.py:155
  541.3 0.2 convolution_convert_fusion.2
  541.5 0.1 copy.44
  541.7 0.1 reshape.375
  541.8 15.4 %all_to_all.33 = bf16[32,2,128]{2,1,0:T(2,128)(2,1)S(1)} all-to-all(bf16[32,2,128]{2,1,0:T(2,128)(2,1)S(1)} %reshape.375), channel_id=1, replica_groups=mesh['dp'=8,'seq'=32] {'seq'}, dimensions={0} | all-to-all | bytes 32768 | tf_op jit(solution)/shard_map/all_to_all | solution.py:159
  557.3 0.1 reshape.369
  557.5 0.1 multiply_reduce_fusion
  557.7 38.6 %all_gather.19 = bf16[256,1024]{1,0:T(8,128)(2,1)S(1)} all-gather(bf16[8,1024]{1,0:T(8,128)(2,1)S(1)} %multiply_convert_fusion), channel_id=1, replica_groups=mesh['dp'=8,'seq'=32] {'seq'}, dimensions={0}, use_global_device_ids=true | all-gather | bytes 540672 | tf_op jit(solution)/shard_map/all_gather | solution.py:165
  596.3 1.3 convolution_convert_fusion
  597.6 109.9 %reduce-scatter.6.cloned.1.call-done = bf16[8,1024]{1,0:T(8,128)(2,1)} async-done(((bf16[256,1024]{1,0:T(8,128)(2,1)}), bf16[8,1024]{1,0:T(8,128)(2,1)}) %reduce-scatter.6.cloned.1.call-update) | async-done | bytes 16400 | tf_op jit(solution)/shard_map/reduce_scatter | solution.py:172
  707.5 1.3 convert_add_fusion
  (50 shorter events, 0.7 us)
Async XLA Ops:
  6.5 77.8 %copy-start = (bf16[1024,1024]{1,0:T(8,128)(2,1)S(1)}, bf16[1024,1024]{1,0:T(8,128)(2,1)}, u32[]{:S(2)}) copy-start(bf16[1024,1024]{1,0:T(8,128)(2,1)} %param.21) | copy-start | bytes 6291460
  6.5 357.5 %reduce-scatter.8.cloned.1.call-start = ((), (), s32[]{:S(2)}) async-start(), calls=%async_computation.6 | async-start | bytes 1081344
  25.9 4.0 copy-start.7
  30.1 5.4 copy-start.5
  30.1 51.8 %copy-start.10 = (f32[32]{0:T(128)S(1)}, f32[32]{0:T(128)}, u32[]{:S(2)}) copy-start(f32[32]{0:T(128)} %constant.77.clone) | copy-start | bytes 388
  30.2 51.8 %copy-start.11 = (s32[32]{0:T(128)S(1)}, s32[32]{0:T(128)}, u32[]{:S(2)}) copy-start(s32[32]{0:T(128)} %constant.80) | copy-start | bytes 388
  35.5 49.8 %copy-start.2 = (f32[1024,1024]{0,1:T(8,128)S(1)}, f32[1024,1024]{0,1:T(8,128)}, u32[]{:S(2)}) copy-start(f32[1024,1024]{0,1:T(8,128)} %copy.37) | copy-start | bytes 12582916
  89.3 5.7 copy-start.1
  223.8 10.1 %copy-start.12 = (u32[256]{0:T(256)S(1)}, u32[256]{0:T(256)}, u32[]{:S(2)}) copy-start(u32[256]{0:T(256)} %constant.85) | copy-start | bytes 3076
  232.5 134.8 %copy-start.8 = (f32[1024]{0:T(1024)S(1)}, f32[1024]{0:T(1024)}, u32[]{:S(2)}) copy-start(f32[1024]{0:T(1024)} %param.24) | copy-start | bytes 12292
  233.8 262.9 %all-gather.2.cloned.1.call-start = ((), (), s32[]{:S(2)}) async-start(), calls=%async_computation.4 | async-start | bytes 1081344 | tf_op jit(solution)/shard_map/all_gather | solution.py:134
  367.3 174.0 %copy-start.6 = (bf16[1024,32]{0,1:T(8,128)(2,1)S(1)}, bf16[1024,32]{0,1:T(8,128)(2,1)}, u32[]{:S(2)}) copy-start(bf16[1024,32]{0,1:T(8,128)(2,1)} %param.26) | copy-start | bytes 196612
  423.0 134.6 %copy-start.9 = (f32[1024]{0:T(1024)S(1)}, f32[1024]{0:T(1024)}, u32[]{:S(2)}) copy-start(f32[1024]{0:T(1024)} %param.27) | copy-start | bytes 12292
  423.8 283.7 %reduce-scatter.6.cloned.1.call-start = ((), (), s32[]{:S(2)}) async-start(), calls=%async_computation.5 | async-start | bytes 540672 | tf_op jit(solution)/shard_map/reduce_scatter | solution.py:172
  424.1 172.2 %copy-start.3 = (bf16[128,1024]{1,0:T(8,128)(2,1)S(1)}, bf16[128,1024]{1,0:T(8,128)(2,1)}, u32[]{:S(2)}) copy-start(bf16[128,1024]{1,0:T(8,128)(2,1)} %param.29) | copy-start | bytes 786436
  499.2 97.1 %copy-start.4 = (bf16[1024,128]{1,0:T(8,128)(2,1)S(1)}, bf16[1024,128]{1,0:T(8,128)(2,1)}, u32[]{:S(2)}) copy-start(bf16[1024,128]{1,0:T(8,128)(2,1)} %param.28) | copy-start | bytes 786436
Sparse Core Ops, SparseCore 0:
  233.9 111.4 reduce-scatter.7
  423.9 72.7 all-gather.1
  597.7 109.7 reduce-scatter.5
where the time goes:
time: 716 us; the launch traced here: 715 us
  blocking collectives  452 us (63%)
  waiting for transfers between devices  183 us (26%)
  matrix products  30.3 us (4%)
  local copies, waits for them, and re-layouts  25.4 us (4%)
  between operations  14.1 us (2%)
  other arithmetic  10.6 us (1%)
    unnamed x1, blocking collectives  129 us
    pmax x1, blocking collectives, on_device(): row_top = lax.pmax(block_peak, 'seq')  129 us
    reduce_scatter x1, waiting for transfers between devices, on_device(): lax.psum_scatter(mlp_terms.astype(jnp.bfloat16), 'seq', scatter_dimension...  110 us
    all_gather x1, waiting for transfers between devices, on_device(): shard_rows = lax.all_gather(owned_key_value, 'seq', axis=0, tiled=True)  72.6 us
    all_gather x1, blocking collectives, on_device(): states_all = lax.all_gather(latent_states, 'seq', axis=0, tiled=True)  46.4 us
    all_gather x1, blocking collectives, on_device(): lax.all_gather(self_mix, 'seq', axis=0, tiled=True)  39.9 us
    all_gather x1, blocking collectives, on_device(): lax.all_gather(normed_mlp, 'seq', axis=0, tiled=True)  38.6 us
    all_gather x1, blocking collectives, on_device(): lax.all_gather(normed, 'seq', axis=0, tiled=True)  37.9 us
  transfers between devices with their start and end apart: 3, of which 2 were waited for; matrix products, arithmetic and copies ran while one was open for 0% of the time, Pallas kernels for 0%

commit v1 on v0

v1 whole, which is shorter than its diff:
```python
import math

import jax
import jax.numpy as jnp
import numpy as np
from jax import lax
from jax.experimental import pallas as pl
from jax.experimental.pallas import tpu as pltpu
from jax.sharding import PartitionSpec as P

F32 = jnp.float32
BF16 = jnp.bfloat16
MESH = pl.DeviceIdType.MESH
LOW = -1e30


def trig_tables():
    periods = np.array([int(4.0 * 16384.0 ** (f / 31)) for f in range(32)], np.int64)

    def angles(positions):
        return 2.0 * np.pi * (positions[None, :] % periods[:, None]) / periods[:, None]

    base = angles(np.arange(1024))
    base = np.concatenate([np.cos(base), np.sin(base)]).astype(np.float32)
    start = angles(np.arange(32) * 1024)
    start = np.concatenate([np.cos(start), np.sin(start)]).astype(np.float32)
    start = np.pad(start, ((0, 0), (0, 96)))
    by_lane = np.tile(periods, 4).astype(np.float64)
    lanes = np.zeros((8, 128), np.float32)
    lanes[0], lanes[1], lanes[2] = by_lane, 1.0 / by_lane, 2.0 * np.pi / by_lane
    return base, start, lanes


def dot(left, right):
    return lax.dot_general(left, right, (((1,), (0,)), ((), ())), preferred_element_type=F32)


def dot_nt(left, right):
    return lax.dot_general(left, right, (((1,), (1,)), ((), ())), preferred_element_type=F32)


def iota(shape, axis):
    return lax.broadcasted_iota(jnp.int32, shape, axis)


def rms_scale(states, gain):
    mean_sq = jnp.mean(states * states, axis=-1, keepdims=True)
    return states * lax.rsqrt(mean_sq + 1e-05) * gain


def kernel(
    ids_ref, states_ref, limits_ref, attn_gain, mlp_gain, qkv_ref, selfo_ref, start_ref, lanes_ref,
    base_hbm, embed_hbm, crossq_hbm, crosskv_hbm, crosso_hbm, up_hbm, down_hbm,
    out_ref,
    crossq, embed, ck, cv, base, crosso, updown_up, updown_dn,
    lim_nat, lim_perm, qsrc, qbuf, ids_all, stpack, strecv, wt, wqkv, selfo,
    acc, peak, packs, comb, mixsrc, mixrecv, mixf, lat, kvall, mix2all, atts, part, precv,
    loc, ss, rs, rs_up, rs_dn, rs_w, rs_kv,
):
    me = lax.axis_index("seq")
    dp = lax.axis_index("dp")
    core = lax.rem(me, 2)
    chip = me // 2
    x = lax.rem(chip, 2)
    z = chip // 2
    quad = lax.rem(me, 4)
    sib = me + 1 - 2 * core
    across = me + 2 - 4 * x
    diagonal = sib + 2 - 4 * x
    dp_pair = dp + 1 - 2 * lax.rem(dp, 2)
    quad_x = quad + 2 - 4 * x

    def same_core(i):
        return lax.rem(chip + i, 16)

    def remote(src, dst, send, recv, seq, part_of=None):
        where = {"seq": seq} if part_of is None else {"dp": part_of, "seq": seq}
        return pltpu.make_async_remote_copy(
            src_ref=src, dst_ref=dst, send_sem=send, recv_sem=recv, device_id=where, device_id_type=MESH
        )

    def over(count, body):
        lax.fori_loop(1, count, lambda i, carry: (body(i), carry)[1], 0)

    barrier = pltpu.get_barrier_semaphore()

    def greet(seq, part_of=None):
        where = {"seq": seq} if part_of is None else {"dp": part_of, "seq": seq}
        pl.semaphore_signal(barrier, inc=1, device_id=where, device_id_type=MESH)

    over(16, lambda i: greet(2 * same_core(i) + core))
    greet(sib)
    greet(diagonal)
    greet(across, dp_pair)

    columns = pl.multiple_of(128 * z, 128)
    local = [
        pltpu.make_async_copy(crossq_hbm, crossq, loc.at[0]),
        pltpu.make_async_copy(embed_hbm, embed, loc.at[1]),
        pltpu.make_async_copy(crosskv_hbm.at[:, pl.ds(columns, 128)], ck, loc.at[2]),
        pltpu.make_async_copy(crosskv_hbm.at[:, pl.ds(columns + 1024, 128)], cv, loc.at[3]),
        pltpu.make_async_copy(base_hbm, base, loc.at[4]),
        pltpu.make_async_copy(up_hbm, updown_up.at[quad], loc.at[5]),
        pltpu.make_async_copy(down_hbm, updown_dn.at[quad], loc.at[6]),
        pltpu.make_async_copy(crosso_hbm, crosso, loc.at[7]),
    ]
    for copy in local:
        copy.start()

    lim_nat[...] = jnp.broadcast_to(limits_ref[...].astype(F32), (128, 256)).T
    for c_of in range(2):
        for x_of in range(2):
            for z_of in range(8):
                slot = ((c_of * 2 + x_of) * 8 + z_of) * 8
                row = (z_of * 4 + x_of * 2 + c_of) * 8
                lim_perm[slot : slot + 8, :] = lim_nat[row : row + 8, :]

    local[0].wait()
    raw = dot(states_ref[...], crossq[...])
    period, inverse, factor = lanes_ref[0:1, :], lanes_ref[1:2, :], lanes_ref[2:3, :]
    position = lim_nat[pl.ds(pl.multiple_of(8 * me, 8), 8), :] - 1.0
    phase = position - jnp.floor(position * inverse) * period
    phase = jnp.where(phase < 0.0, phase + period, phase)
    phase = jnp.where(phase >= period, phase - period, phase) * factor
    lane8 = iota((8, 128), 1)
    first = lax.rem(lane8, 64) < 32
    cosines = jnp.cos(phase)
    sines = jnp.sin(phase)
    sines = jnp.where(first, -sines, sines)
    for p in range(8):
        tile = raw[:, 128 * p : 128 * p + 128]
        swapped = jnp.where(first, pltpu.roll(tile, 96, 1), pltpu.roll(tile, 32, 1))
        qsrc[p] = (tile * cosines + swapped * sines).astype(BF16).astype(F32) * 0.125
    qbuf[core, x * 8 + z] = qsrc[z]
    ids_all[chip] = ids_ref[...]
    packed = states_ref[...].astype(F32)
    packed = jnp.concatenate([packed[:, :512], packed[:, 512:]], axis=0).astype(BF16)
    stpack[...] = packed
    strecv[z] = packed

    pl.semaphore_wait(barrier, 18)

    def send_ids(i):
        k = same_core(i)
        remote(ids_ref, ids_all.at[chip], ss.at[0], rs.at[0], 2 * k + core).start()
        remote(qsrc.at[k // 2], qbuf.at[core, x * 8 + z], ss.at[1], rs.at[1], 2 * k + core).start()

    over(16, send_ids)

    def ring(i):
        return lax.rem(me + 4 * i, 32)

    over(8, lambda i: remote(stpack, strecv.at[z], ss.at[2], rs.at[2], ring(i)).start())
    own_up = [
        remote(up_hbm, updown_up.at[quad], ss.at[3], rs_up.at[quad], sib),
        remote(down_hbm, updown_dn.at[quad], ss.at[4], rs_dn.at[quad], sib),
        remote(up_hbm, updown_up.at[quad], ss.at[5], rs_up.at[quad], across, dp_pair),
        remote(down_hbm, updown_dn.at[quad], ss.at[6], rs_dn.at[quad], across, dp_pair),
    ]
    for copy in own_up:
        copy.start()

    eye = (iota((128, 128), 0) == iota((128, 128), 1)).astype(F32).astype(BF16)
    both = jnp.concatenate([qkv_ref[...], selfo_ref[...]], axis=1)
    wt[...] = dot_nt(eye, both).astype(BF16).reshape(4, 32, 1024)
    selfo[chip, core] = wt[3]

    def unit_copies(i, x_of):
        unit = 3 * me + i
        index = 4 * (unit // 32) + lax.rem(unit, 4)
        target = 4 * (lax.rem(unit, 32) // 4) + 2 * x_of + core
        away = remote(wt.at[i], wqkv.at[index], ss.at[7 + 2 * i + x_of], rs_w.at[index], target)
        here = pltpu.make_async_copy(wt.at[i], wqkv.at[index], rs_w.at[index])
        return target, away, here

    for i in range(3):
        for x_of in range(2):
            target, away, here = unit_copies(i, x_of)
            pl.when(target != me)(away.start)
            pl.when(target == me)(here.start)

    over(
        16,
        lambda i: remote(
            wt.at[3], selfo.at[chip, core], ss.at[13], rs.at[3], 2 * same_core(i) + core
        ).start(),
    )

    local[1].wait()
    local[2].wait()
    local[3].wait()
    local[4].wait()
    key_rows = dot(embed[...], ck[...]).T
    key_rows = jnp.where(x == 0, key_rows[0:64], key_rows[64:128])
    value_rows = dot(embed[...], cv[...]).T
    value_rows = jnp.where(x == 0, value_rows[0:64], value_rows[64:128])
    key_top = key_rows.astype(BF16)
    key_rest = (key_rows - key_top.astype(F32)).astype(BF16)
    table = jnp.concatenate([key_top, key_rest, value_rows.astype(BF16)], axis=0)

    def wait_in(buf, sem):
        pltpu.make_async_copy(buf, buf, sem).wait()

    wait_in(ids_all.at[pl.ds(0, 15)], rs.at[0])
    wait_in(qbuf.at[core, pl.ds(0, 15)], rs.at[1])
    forward_q = remote(qbuf.at[core], qbuf.at[core], ss.at[14], rs.at[4], sib)
    forward_q.start()
    wait_in(qbuf.at[1 - core], rs.at[4])
    lane256 = iota((256, 128), 1)
    queries = jnp.where(lane256 // 64 == x, qbuf[...].reshape(256, 128), 0.0).astype(BF16)
    acc[...] = jnp.zeros((256, 128), F32)
    peak[...] = jnp.full((256, 128), LOW, F32)

    def context_block(j, masked):
        block = 2 * j + core
        onehot = (iota((256, 1024), 0) == ids_all[j]).astype(F32).astype(BF16)
        rows = dot(table, onehot)
        keys = rows[0:64] + rows[64:128]
        here = jnp.where(iota((64, 128), 1) == block, start_ref[...], 0.0)
        here = jnp.sum(here, axis=1, keepdims=True)
        cos_a, sin_a, cos_b, sin_b = here[0:32], here[32:64], base[0:32, :], base[32:64, :]
        cos = cos_a * cos_b - sin_a * sin_b
        sin = sin_a * cos_b + cos_a * sin_b
        one, two = keys[0:32], keys[32:64]
        turned = jnp.concatenate([one * cos - two * sin, two * cos + one * sin], axis=0)
        turned = turned.astype(BF16)
        scores = dot(queries, jnp.concatenate([turned, turned], axis=0))
        if masked:
            place = (block * 1024 + iota((1, 1024), 1)).astype(F32)
            scores = jnp.where(place < lim_perm[:, 0:1], scores, LOW)
        top = jnp.max(scores, axis=1, keepdims=True)
        weights = jnp.exp(scores - top).astype(BF16)
        values = jnp.concatenate([rows[128:192].astype(BF16), jnp.ones((64, 1024), BF16)], axis=0)
        terms = dot_nt(weights, values)
        old = peak[...]
        new = jnp.maximum(old, top)
        acc[...] = acc[...] * jnp.exp(old - new) + terms * jnp.exp(top - new)
        peak[...] = new

    lax.fori_loop(0, 8, lambda j, carry: (context_block(j, False), carry)[1], 0)
    lax.fori_loop(8, 16, lambda j, carry: (context_block(j, True), carry)[1], 0)

    packs[...] = jnp.where(lane256 == 127, peak[...], acc[...]).reshape(2, 128, 128)
    swap = remote(packs.at[1 - core], comb, ss.at[15], rs.at[5], sib)
    swap.start()

    wait_in(updown_up.at[quad_x], rs_up.at[quad_x])
    wait_in(updown_dn.at[quad_x], rs_dn.at[quad_x])
    forwards = [
        remote(updown_up.at[quad_x], updown_up.at[quad_x], ss.at[16], rs_up.at[quad_x], sib),
        remote(updown_dn.at[quad_x], updown_dn.at[quad_x], ss.at[17], rs_dn.at[quad_x], sib),
    ]
    for copy in forwards:
        copy.start()

    def unit_core(index):
        unit = 32 * (index // 4) + 4 * z + index % 4
        return lax.rem(unit // 3, 2)

    def unit_forward(index):
        return remote(wqkv.at[index], wqkv.at[index], ss.at[18 + index], rs_w.at[index], sib)

    def pass_unit(index):
        wait_in(wqkv.at[index], rs_w.at[index])
        unit_forward(index).start()

    for index in range(12):
        pl.when(unit_core(index) == core)(lambda index=index: pass_unit(index))

    wait_in(comb, rs.at[5])
    mine, theirs = packs[core], comb[...]
    peak_a, peak_b = mine[:, 127:128], theirs[:, 127:128]
    top = jnp.maximum(peak_a, peak_b)
    both = mine * jnp.exp(peak_a - top) + theirs * jnp.exp(peak_b - top)
    mixed = both / both[:, 64:65]
    lane32 = iota((32, 128), 1)
    for x_of in range(2):
        low, high = mixed[64 * x_of : 64 * x_of + 32], mixed[64 * x_of + 32 : 64 * x_of + 64]
        mixsrc[x_of] = jnp.where(lane32 < 64, low, pltpu.roll(high, 64, 1)).astype(BF16)
    mixrecv[chip] = mixsrc[x]

    def send_mix(i):
        k = same_core(i)
        remote(mixsrc.at[lax.rem(k, 2)], mixrecv.at[chip], ss.at[30], rs.at[6], 2 * k + core).start()

    over(16, send_mix)

    wait_in(selfo.at[pl.ds(0, 15), 0], rs.at[3])
    forward_o = remote(selfo.at[:, core], selfo.at[:, core], ss.at[31], rs.at[7], sib)
    forward_o.start()

    wait_in(strecv.at[pl.ds(0, 7)], rs.at[2])
    for z_of in range(8):
        rows = strecv[z_of].astype(F32)
        lat[8 * z_of : 8 * z_of + 8, :] = jnp.concatenate([rows[0:8], rows[8:16]], axis=1)
    for index in range(12):
        pl.when(unit_core(index) != core)(
            lambda index=index: wait_in(wqkv.at[index], rs_w.at[index])
        )
    local[7].wait()
    wait_in(mixrecv.at[pl.ds(0, 15)], rs.at[6])
    for p in range(8):
        even, odd = mixrecv[2 * p].astype(F32), mixrecv[2 * p + 1].astype(F32)
        above = jnp.where(lane32 < 64, even, pltpu.roll(odd, 64, 1))
        below = jnp.where(lane32 < 64, pltpu.roll(even, 64, 1), odd)
        mixf[:, 128 * p : 128 * p + 128] = jnp.concatenate([above, below], axis=0).astype(BF16)
    latents = lat[...] + dot(mixf[...], crosso[...])
    normed = rms_scale(latents, attn_gain[...]).astype(BF16)
    lat[...] = latents

    projected = dot_nt(normed, wqkv[...].reshape(384, 1024)).astype(BF16)
    kvall[quad] = projected[:, 128:384]
    kv_copies = [
        remote(kvall.at[quad], kvall.at[quad], ss.at[32 + n], rs_kv.at[quad], seq)
        for n, seq in enumerate((sib, across, diagonal))
    ]
    for copy in kv_copies:
        copy.start()
    for other in (1, 2, 3):
        slot = lax.rem(quad + other, 4)
        wait_in(kvall.at[slot], rs_kv.at[slot])
    lane64 = iota((64, 128), 1)
    keys = kvall[:, :, 0:128].reshape(256, 128)
    values = kvall[:, :, 128:256].reshape(256, 128)
    key_lane = iota((64, 256), 1)
    key_row = 32 * (lax.rem(key_lane, 64) // 8) + 8 * (key_lane // 64) + lax.rem(key_lane, 8)
    query_at = iota((64, 256), 0)
    query_row = 32 * (query_at // 8) + 8 * quad + lax.rem(query_at, 8)
    causal = key_row <= query_row
    heads = []
    for head in range(2):
        only = jnp.where(lane64 // 64 == head, projected[:, 0:128].astype(F32), 0.0).astype(BF16)
        scores = jnp.where(causal, dot_nt(only, keys) * 0.125, LOW)
        weights = jnp.exp(scores - jnp.max(scores, axis=1, keepdims=True))
        total = jnp.sum(weights, axis=1, keepdims=True)
        coarse = weights.astype(BF16)
        fine = (weights - coarse.astype(F32)).astype(BF16)
        heads.append((dot(coarse, values) + dot(fine, values)) / total)
    mix2all[z] = jnp.where(lane64 < 64, heads[0], heads[1]).astype(BF16)
    over(8, lambda i: remote(mix2all.at[z], mix2all.at[z], ss.at[35], rs.at[8], ring(i)).start())
    wait_in(selfo.at[:, 1 - core], rs.at[7])
    wait_in(mix2all.at[pl.ds(0, 7)], rs.at[8])
    mix2 = jnp.concatenate([mix2all[k] for k in range(8)], axis=1)
    attended = lat[...] + dot_nt(mix2, selfo[...].reshape(1024, 1024))
    atts[...] = attended.reshape(8, 8, 1024)
    normed = rms_scale(attended, mlp_gain[...]).astype(BF16)

    local[5].wait()
    local[6].wait()
    for slot in (quad + 1 - 2 * core, quad_x + 1 - 2 * core):
        wait_in(updown_up.at[slot], rs_up.at[slot])
        wait_in(updown_dn.at[slot], rs_dn.at[slot])
    hidden = []
    for half in range(2):
        ups = jnp.concatenate([updown_up[2 * half], updown_up[2 * half + 1]], axis=1)
        hidden.append(jax.nn.gelu(dot(normed, ups), approximate=True).astype(BF16))
    hidden = jnp.concatenate(hidden, axis=1)
    part[...] = dot(hidden, updown_dn[...].reshape(512, 1024)).reshape(8, 8, 1024)
    precv[z] = part[z]

    def send_part(i):
        seq = ring(i)
        remote(part.at[seq // 4], precv.at[z], ss.at[36], rs.at[9], seq).start()

    over(8, send_part)
    wait_in(precv.at[pl.ds(0, 7)], rs.at[9])
    total = atts[z]
    summed = precv[0]
    for k in range(1, 8):
        summed = summed + precv[k]
    out_ref[...] = total + summed

    def wait_out(buf, sem):
        pltpu.make_async_copy(buf, buf, sem).wait()

    wait_out(ids_all.at[pl.ds(0, 15)], ss.at[0])
    wait_out(qbuf.at[0, pl.ds(0, 15)], ss.at[1])
    wait_out(strecv.at[pl.ds(0, 7)], ss.at[2])
    for copy in own_up + forwards + kv_copies + [forward_q, swap, forward_o]:
        copy.wait_send()
    for i in range(3):
        for x_of in range(2):
            target, away, _ = unit_copies(i, x_of)
            pl.when(target != me)(away.wait_send)
    for index in range(12):
        pl.when(unit_core(index) == core)(lambda index=index: unit_forward(index).wait_send())
    wait_out(selfo.at[pl.ds(0, 15), 0], ss.at[13])
    wait_out(mixrecv.at[pl.ds(0, 15)], ss.at[30])
    wait_out(mix2all.at[pl.ds(0, 7)], ss.at[35])
    wait_out(precv.at[pl.ds(0, 7)], ss.at[36])


def on_device(
    context_ids, embed_table, latent_states, limits, cross_q, cross_kv, cross_o,
    attn_gain, self_qkv, self_o, mlp_gain, mlp_up, mlp_down,
):
    base, start, lanes = trig_tables()
    vmem = pl.BlockSpec(memory_space=pltpu.VMEM)
    anywhere = pl.BlockSpec(memory_space=pl.ANY)
    dma = pltpu.SemaphoreType.DMA
    return pl.pallas_call(
        kernel,
        out_shape=jax.ShapeDtypeStruct((8, 1024), F32),
        in_specs=[vmem] * 9 + [anywhere] * 7,
        out_specs=vmem,
        scratch_shapes=[
            pltpu.VMEM((1024, 1024), BF16),
            pltpu.VMEM((256, 1024), BF16),
            pltpu.VMEM((1024, 128), BF16),
            pltpu.VMEM((1024, 128), BF16),
            pltpu.VMEM((64, 1024), F32),
            pltpu.VMEM((1024, 1024), BF16),
            pltpu.VMEM((4, 1024, 128), BF16),
            pltpu.VMEM((4, 128, 1024), BF16),
            pltpu.VMEM((256, 128), F32),
            pltpu.VMEM((256, 128), F32),
            pltpu.VMEM((8, 8, 128), F32),
            pltpu.VMEM((2, 16, 8, 128), F32),
            pltpu.VMEM((16, 1, 1024), jnp.int32),
            pltpu.VMEM((16, 512), BF16),
            pltpu.VMEM((8, 16, 512), BF16),
            pltpu.VMEM((4, 32, 1024), BF16),
            pltpu.VMEM((12, 32, 1024), BF16),
            pltpu.VMEM((16, 2, 32, 1024), BF16),
            pltpu.VMEM((256, 128), F32),
            pltpu.VMEM((256, 128), F32),
            pltpu.VMEM((2, 128, 128), F32),
            pltpu.VMEM((128, 128), F32),
            pltpu.VMEM((2, 32, 128), BF16),
            pltpu.VMEM((16, 32, 128), BF16),
            pltpu.VMEM((64, 1024), BF16),
            pltpu.VMEM((64, 1024), F32),
            pltpu.VMEM((4, 64, 256), BF16),
            pltpu.VMEM((8, 64, 128), BF16),
            pltpu.VMEM((8, 8, 1024), F32),
            pltpu.VMEM((8, 8, 1024), F32),
            pltpu.VMEM((8, 8, 1024), F32),
            dma((8,)),
            dma((37,)),
            dma((10,)),
            dma((4,)),
            dma((4,)),
            dma((12,)),
            dma((4,)),
        ],
        compiler_params=pltpu.CompilerParams(
            collective_id=0, has_side_effects=True, vmem_limit_bytes=48 << 20
        ),
        name="ar_step",
    )(
        context_ids.reshape(1, -1), latent_states, limits.reshape(1, -1),
        attn_gain.reshape(1, -1), mlp_gain.reshape(1, -1), self_qkv, self_o,
        jnp.asarray(start), jnp.asarray(lanes), jnp.asarray(base),
        embed_table, cross_q, cross_kv, cross_o, mlp_up, mlp_down,
    )


def solution(mesh):
    placed = (
        P(("dp", "seq")),
        P(),
        P(("dp", "seq"), None),
        P("dp"),
        P(),
        P(),
        P(),
        P(),
        P(None, "seq"),
        P(None, "seq"),
        P(),
        P(None, "seq"),
        P("seq", None),
    )
    return jax.shard_map(
        on_device, mesh=mesh, in_specs=placed, out_specs=P(("dp", "seq"), None), check_vma=False
    )
```

time: 716 us -> 95.1 us (0.13)
  blocking collectives: 452 us -> 0 us
  waiting for transfers between devices: 183 us -> 0 us
  Pallas kernels: 0 us -> 79.8 us
  matrix products: 30.3 us -> 0 us
  between operations: 14.1 us -> 0.04 us
  local copies, waits for them, and re-layouts: 25.4 us -> 14.7 us
  other arithmetic: 10.6 us -> 0 us
    all_gather x4 -> x0, blocking collectives: 163 us -> none  [the longest x1 46.4 us: on_device(): states_all = lax.all_gather(latent_states, 'seq', axis=0, tiled=True)]
    unnamed x1 -> x0, blocking collectives: 129 us -> none
    pmax x1 -> x0, blocking collectives: 129 us -> none  [on_device(): row_top = lax.pmax(block_peak, 'seq')]
    reduce_scatter x1 -> x0, waiting for transfers between devices: 110 us -> none  [on_device(): lax.psum_scatter(mlp_terms.astype(jnp.bfloat16), 'seq', scatter_dimension...]
    pallas_call x0 -> x1, Pallas kernels: none -> 79.8 us  [on_device(): pl.pallas_call(kernel, out_shape=jax.ShapeDtypeStruct((8, 1024), F32), in...]
    all_gather x1 -> x0, waiting for transfers between devices: 72.6 us -> none  [on_device(): shard_rows = lax.all_gather(owned_key_value, 'seq', axis=0, tiled=True)]
    all_to_all x2 -> x0, blocking collectives: 31.8 us -> none  [the longest x1 16.4 us: on_device(): lax.all_to_all(column_part, 'seq', split_axis=0, concat_axis=1, tiled=True)]
    dot_general x10 -> x0, matrix products: 30.3 us -> none  [the longest x1 10.8 us: on_device(): key_value = jnp.dot(embedded, cross_kv, preferred_element_type=jnp.float32)]
  transfers between devices with their start and end apart: 3 -> 0, of which waited for: 2 -> 0; matrix products, arithmetic and copies ran while one was open for 0% -> 0% of each run, Pallas kernels for 0% -> 0%
where the time goes in v1:
time: 95.1 us; the launch traced here: 94.5 us
  Pallas kernels  79.8 us (84%)
  local copies, waits for them, and re-layouts  14.7 us (15%)
    pallas_call x1, Pallas kernels, on_device(): pl.pallas_call(kernel, out_shape=jax.ShapeDtypeStruct((8, 1024), F32), in...  79.8 us
    unnamed x29, local copies, waits for them, and re-layouts  14.7 us

profile of v1, /device:TPU:16, one launch (start us, length us, event | category | flops | bytes accessed | tf_op | source)
XLA Modules:
  0.0 94.5 jit_solution(14787333068007649287)
XLA Ops:
  0.0 1.1 %copy.17.qkv_ref = bf16[1024,96]{1,0:T(8,128)(2,1)S(1)} copy(bf16[1024,96]{0,1:T(8,128)(2,1)} %param.24) | data formatting | bytes 393216 | tf_op args[8]
  1.1 1.0 %copy.18.selfo_ref = bf16[1024,32]{1,0:T(8,128)(2,1)S(1)} copy(bf16[1024,32]{0,1:T(8,128)(2,1)} %param.25) | data formatting | bytes 131072 | tf_op args[9]
  2.1 0.0 copy-start
  2.1 1.6 %copy-done = bf16[1024,1024]{1,0:T(8,128)(2,1)S(1)} copy-done((bf16[1024,1024]{1,0:T(8,128)(2,1)S(1)}, bf16[1024,1024]{1,0:T(8,128)(2,1)}, u32[]{:S(2)}) %copy-start) | copy-done | bytes 2097176
  3.7 0.0 copy-start.1
  3.7 1.6 %copy-done.1 = bf16[1024,1024]{1,0:T(8,128)(2,1)S(1)} copy-done((bf16[1024,1024]{1,0:T(8,128)(2,1)S(1)}, bf16[1024,1024]{1,0:T(8,128)(2,1)}, u32[]{:S(2)}) %copy-start.1) | copy-done | bytes 2097176
  5.3 0.0 copy-start.2
  5.3 1.0 %copy-done.2 = bf16[256,1024]{1,0:T(8,128)(2,1)S(1)} copy-done((bf16[256,1024]{1,0:T(8,128)(2,1)S(1)}, bf16[256,1024]{1,0:T(8,128)(2,1)}, u32[]{:S(2)}) %copy-start.2) | copy-done | bytes 524312
  6.3 0.0 copy-start.3
  6.4 0.9 %copy-done.3 = bf16[1024,128]{1,0:T(8,128)(2,1)S(1)} copy-done((bf16[1024,128]{1,0:T(8,128)(2,1)S(1)}, bf16[1024,128]{1,0:T(8,128)(2,1)}, u32[]{:S(2)}) %copy-start.3) | copy-done | bytes 262168
  7.3 0.0 copy-start.4
  7.3 0.9 %copy-done.4 = bf16[128,1024]{1,0:T(8,128)(2,1)S(1)} copy-done((bf16[128,1024]{1,0:T(8,128)(2,1)S(1)}, bf16[128,1024]{1,0:T(8,128)(2,1)}, u32[]{:S(2)}) %copy-start.4) | copy-done | bytes 262168
  8.2 0.0 copy-start.5
  8.3 0.9 %copy-done.5 = f32[64,1024]{1,0:T(8,128)S(1)} copy-done((f32[64,1024]{1,0:T(8,128)S(1)}, f32[64,1024]{1,0:T(8,128)}, u32[]{:S(2)}) %copy-start.5) | copy-done | bytes 262168
  9.2 0.0 copy-start.6
  9.2 0.8 copy-done.6
  10.0 0.0 copy-start.7
  10.0 0.7 copy-done.7
  10.7 0.0 copy-start.8
  10.7 0.7 copy-done.8
  11.4 0.0 copy-start.9
  11.4 0.7 copy-done.9
  12.1 0.0 copy-start.10
  12.1 0.7 copy-done.10
  12.7 0.0 copy-start.11
  12.7 0.7 copy-done.11
  13.4 0.0 copy-start.12
  13.4 0.7 copy-done.12
  14.1 79.8 %ar_step.1 = f32[8,1024]{1,0:T(8,128)S(1)} custom-call(s32[1,1024]{1,0:T(1,128)S(1)} %bitcast.4, bf16[8,1024]{1,0:T(8,128)(2,1)S(1)} %copy-done.7, s32[1,256]{1,0:T(1,128)S(1)} %bitcast.7, f32[1,1024]{1,0:T(1,128)S(1)} %bitcast.5, f32[1,1024]{1,0:T(1,128)S(1)} %bitcast.6, bf16[1024,96]{1,0:T(8,128)(2,1)S(1)} %copy.17.qkv_ref, ...), custom_call_target="tpu_custom_call" | custom-call | tf_op jit(solution)/shard_map/ar_step/pallas_call | solution.py:401
  93.9 0.6 copy.20
Async XLA Ops:
  2.1 1.6 %copy-start = (bf16[1024,1024]{1,0:T(8,128)(2,1)S(1)}, bf16[1024,1024]{1,0:T(8,128)(2,1)}, u32[]{:S(2)}) copy-start(bf16[1024,1024]{1,0:T(8,128)(2,1)} %crossq_hbm.1) | copy-start | bytes 6291460
  3.7 1.6 %copy-start.1 = (bf16[1024,1024]{1,0:T(8,128)(2,1)S(1)}, bf16[1024,1024]{1,0:T(8,128)(2,1)}, u32[]{:S(2)}) copy-start(bf16[1024,1024]{1,0:T(8,128)(2,1)} %crosso_hbm.1) | copy-start | bytes 6291460
  5.3 1.0 %copy-start.2 = (bf16[256,1024]{1,0:T(8,128)(2,1)S(1)}, bf16[256,1024]{1,0:T(8,128)(2,1)}, u32[]{:S(2)}) copy-start(bf16[256,1024]{1,0:T(8,128)(2,1)} %embed_hbm.1) | copy-start | bytes 1572868
  6.3 0.9 %copy-start.3 = (bf16[1024,128]{1,0:T(8,128)(2,1)S(1)}, bf16[1024,128]{1,0:T(8,128)(2,1)}, u32[]{:S(2)}) copy-start(bf16[1024,128]{1,0:T(8,128)(2,1)} %up_hbm.1) | copy-start | bytes 786436
  7.3 0.9 %copy-start.4 = (bf16[128,1024]{1,0:T(8,128)(2,1)S(1)}, bf16[128,1024]{1,0:T(8,128)(2,1)}, u32[]{:S(2)}) copy-start(bf16[128,1024]{1,0:T(8,128)(2,1)} %down_hbm.1) | copy-start | bytes 786436
  8.2 0.9 %copy-start.5 = (f32[64,1024]{1,0:T(8,128)S(1)}, f32[64,1024]{1,0:T(8,128)}, u32[]{:S(2)}) copy-start(f32[64,1024]{1,0:T(8,128)} %constant.8.clone.base_hbm) | copy-start | bytes 786436
  9.2 0.8 copy-start.6
  10.0 0.7 copy-start.7
  10.7 0.7 copy-start.8
  11.4 0.7 copy-start.9
  12.1 0.7 copy-start.10
  12.7 0.7 copy-start.11
  13.4 0.7 copy-start.12

commit v2 on v1

--- a/solution.py
+++ b/solution.py
@@ -49,9 +49,10 @@
 
 
 def kernel(
-    ids_ref, states_ref, limits_ref, attn_gain, mlp_gain, qkv_ref, selfo_ref, start_ref, lanes_ref,
+    ids_hbm, states_hbm, limits_hbm, attn_gain_hbm, mlp_gain_hbm, qkv_hbm, selfo_hbm, start_hbm, lanes_hbm,
     base_hbm, embed_hbm, crossq_hbm, crosskv_hbm, crosso_hbm, up_hbm, down_hbm,
     out_ref,
+    ids_ref, states_ref, limits_ref, attn_gain, mlp_gain, start_ref, lanes_ref,
     crossq, embed, ck, cv, base, crosso, updown_up, updown_dn,
     lim_nat, lim_perm, qsrc, qbuf, ids_all, stpack, strecv, wt, wqkv, selfo,
     acc, peak, packs, comb, mixsrc, mixrecv, mixf, lat, kvall, mix2all, atts, part, precv,
@@ -68,6 +69,8 @@
     across = me + 2 - 4 * x
     diagonal = sib + 2 - 4 * x
     dp_pair = dp + 1 - 2 * lax.rem(dp, 2)
+    y = dp // 2
+    carrier = lax.rem(z, 4) == y
     quad_x = quad + 2 - 4 * x
 
     def same_core(i):
@@ -92,6 +95,7 @@
     greet(sib)
     greet(diagonal)
     greet(across, dp_pair)
+    over(4, lambda i: greet(me, lax.rem(dp + 2 * i, 8)))
 
     columns = pl.multiple_of(128 * z, 128)
     local = [
@@ -103,9 +107,21 @@
         pltpu.make_async_copy(up_hbm, updown_up.at[quad], loc.at[5]),
         pltpu.make_async_copy(down_hbm, updown_dn.at[quad], loc.at[6]),
         pltpu.make_async_copy(crosso_hbm, crosso, loc.at[7]),
+        pltpu.make_async_copy(ids_hbm, ids_ref, loc.at[8]),
+        pltpu.make_async_copy(states_hbm, states_ref, loc.at[9]),
+        pltpu.make_async_copy(limits_hbm, limits_ref, loc.at[10]),
+        pltpu.make_async_copy(attn_gain_hbm, attn_gain, loc.at[11]),
+        pltpu.make_async_copy(mlp_gain_hbm, mlp_gain, loc.at[12]),
+        pltpu.make_async_copy(start_hbm, start_ref, loc.at[13]),
+        pltpu.make_async_copy(lanes_hbm, lanes_ref, loc.at[14]),
+        pltpu.make_async_copy(qkv_hbm, wt.at[pl.ds(0, 96)], loc.at[15]),
+        pltpu.make_async_copy(selfo_hbm, wt.at[pl.ds(96, 32)], loc.at[16]),
     ]
     for copy in local:
         copy.start()
+
+    for n in (10, 9, 8, 14):
+        local[n].wait()
 
     lim_nat[...] = jnp.broadcast_to(limits_ref[...].astype(F32), (128, 256)).T
     for c_of in range(2):
@@ -138,7 +154,7 @@
     stpack[...] = packed
     strecv[z] = packed
 
-    pl.semaphore_wait(barrier, 18)
+    pl.semaphore_wait(barrier, 21)
 
     def send_ids(i):
         k = same_core(i)
@@ -151,6 +167,16 @@
         return lax.rem(me + 4 * i, 32)
 
     over(8, lambda i: remote(stpack, strecv.at[z], ss.at[2], rs.at[2], ring(i)).start())
+    local[16].wait()
+
+    def send_selfo(i):
+        remote(wt.at[pl.ds(96, 32)], selfo.at[chip, core], ss.at[13], rs.at[3], ring(i)).start()
+
+    @pl.when(carrier)
+    def _():
+        selfo[chip, core] = wt[96:128, :]
+        over(8, send_selfo)
+
     own_up = [
         remote(up_hbm, updown_up.at[quad], ss.at[3], rs_up.at[quad], sib),
         remote(down_hbm, updown_dn.at[quad], ss.at[4], rs_dn.at[quad], sib),
@@ -160,36 +186,11 @@
     for copy in own_up:
         copy.start()
 
-    eye = (iota((128, 128), 0) == iota((128, 128), 1)).astype(F32).astype(BF16)
-    both = jnp.concatenate([qkv_ref[...], selfo_ref[...]], axis=1)
-    wt[...] = dot_nt(eye, both).astype(BF16).reshape(4, 32, 1024)
-    selfo[chip, core] = wt[3]
-
-    def unit_copies(i, x_of):
-        unit = 3 * me + i
-        index = 4 * (unit // 32) + lax.rem(unit, 4)
-        target = 4 * (lax.rem(unit, 32) // 4) + 2 * x_of + core
-        away = remote(wt.at[i], wqkv.at[index], ss.at[7 + 2 * i + x_of], rs_w.at[index], target)
-        here = pltpu.make_async_copy(wt.at[i], wqkv.at[index], rs_w.at[index])
-        return target, away, here
-
-    for i in range(3):
-        for x_of in range(2):
-            target, away, here = unit_copies(i, x_of)
-            pl.when(target != me)(away.start)
-            pl.when(target == me)(here.start)
-
-    over(
-        16,
-        lambda i: remote(
-            wt.at[3], selfo.at[chip, core], ss.at[13], rs.at[3], 2 * same_core(i) + core
-        ).start(),
-    )
-
     local[1].wait()
     local[2].wait()
     local[3].wait()
     local[4].wait()
+    local[13].wait()
     key_rows = dot(embed[...], ck[...]).T
     key_rows = jnp.where(x == 0, key_rows[0:64], key_rows[64:128])
     value_rows = dot(embed[...], cv[...]).T
@@ -206,6 +207,22 @@
     forward_q = remote(qbuf.at[core], qbuf.at[core], ss.at[14], rs.at[4], sib)
     forward_q.start()
     wait_in(qbuf.at[1 - core], rs.at[4])
+
+    local[15].wait()
+
+    def unit_copies(i):
+        unit = 3 * me + i
+        index = 4 * (unit // 32) + lax.rem(unit, 4)
+        target = 4 * (lax.rem(unit, 32) // 4) + quad
+        away = remote(wt.at[pl.ds(32 * i, 32)], wqkv.at[index], ss.at[7 + i], rs_w.at[index], target)
+        here = pltpu.make_async_copy(wt.at[pl.ds(32 * i, 32)], wqkv.at[index], rs_w.at[index])
+        return target, away, here
+
+    for i in range(3):
+        target, away, here = unit_copies(i)
+        pl.when(target != me)(away.start)
+        pl.when(target == me)(here.start)
+
     lane256 = iota((256, 128), 1)
     queries = jnp.where(lane256 // 64 == x, qbuf[...].reshape(256, 128), 0.0).astype(BF16)
     acc[...] = jnp.zeros((256, 128), F32)
@@ -237,8 +254,55 @@
         acc[...] = acc[...] * jnp.exp(old - new) + terms * jnp.exp(top - new)
         peak[...] = new
 
-    lax.fori_loop(0, 8, lambda j, carry: (context_block(j, False), carry)[1], 0)
-    lax.fori_loop(8, 16, lambda j, carry: (context_block(j, True), carry)[1], 0)
+    lax.fori_loop(0, 8, lambda j, carry: (context_block(j, False), carry)[1], 0, unroll=4)
+
+    lax.fori_loop(8, 12, lambda j, carry: (context_block(j, True), carry)[1], 0, unroll=4)
+
+    @pl.when(carrier)
+    def _():
+        wait_in(selfo.at[pl.ds(0, 1), 0], rs.at[3])
+
+    @pl.when(jnp.logical_not(carrier))
+    def _():
+        wait_in(selfo.at[pl.ds(0, 2), 0], rs.at[3])
+
+    along_x = []
+    for n in range(2):
+        brought = selfo.at[2 * y + 8 * n + x, core]
+        along_x.append(remote(brought, brought, ss.at[43 + n], rs.at[11], across, dp_pair))
+    for copy in along_x:
+        copy.start()
+
+    def unit_quad(index):
+        unit = 32 * (index // 4) + 4 * z + index % 4
+        return lax.rem(unit // 3, 4)
+
+    def unit_across(index):
+        return remote(wqkv.at[index], wqkv.at[index], ss.at[45 + index], rs_w.at[index], across, dp_pair)
+
+    def unit_forward(index):
+        return remote(wqkv.at[index], wqkv.at[index], ss.at[18 + index], rs_w.at[index], sib)
+
+    def turn_unit(index):
+        wait_in(wqkv.at[index], rs_w.at[index])
+        unit_across(index).start()
+        unit_forward(index).start()
+
+    for index in range(12):
+        pl.when(unit_quad(index) == quad)(lambda index=index: turn_unit(index))
+
+    lax.fori_loop(12, 16, lambda j, carry: (context_block(j, True), carry)[1], 0, unroll=4)
+
+    wait_in(selfo.at[pl.ds(0, 2), 0], rs.at[11])
+    along_y = []
+    for i in range(1, 4):
+        for n in range(2):
+            brought = selfo.at[pl.ds(2 * y + 8 * n, 2), core]
+            sem = ss.at[37 + 2 * (i - 1) + n]
+            along_y.append(remote(brought, brought, sem, rs.at[10], me, lax.rem(dp + 2 * i, 8)))
+    for copy in along_y:
+        copy.start()
+
 
     packs[...] = jnp.where(lane256 == 127, peak[...], acc[...]).reshape(2, 128, 128)
     swap = remote(packs.at[1 - core], comb, ss.at[15], rs.at[5], sib)
@@ -253,19 +317,12 @@
     for copy in forwards:
         copy.start()
 
-    def unit_core(index):
-        unit = 32 * (index // 4) + 4 * z + index % 4
-        return lax.rem(unit // 3, 2)
-
-    def unit_forward(index):
-        return remote(wqkv.at[index], wqkv.at[index], ss.at[18 + index], rs_w.at[index], sib)
-
     def pass_unit(index):
         wait_in(wqkv.at[index], rs_w.at[index])
         unit_forward(index).start()
 
     for index in range(12):
-        pl.when(unit_core(index) == core)(lambda index=index: pass_unit(index))
+        pl.when(unit_quad(index) == quad_x)(lambda index=index: pass_unit(index))
 
     wait_in(comb, rs.at[5])
     mine, theirs = packs[core], comb[...]
@@ -285,19 +342,17 @@
 
     over(16, send_mix)
 
-    wait_in(selfo.at[pl.ds(0, 15), 0], rs.at[3])
-    forward_o = remote(selfo.at[:, core], selfo.at[:, core], ss.at[31], rs.at[7], sib)
-    forward_o.start()
-
     wait_in(strecv.at[pl.ds(0, 7)], rs.at[2])
     for z_of in range(8):
         rows = strecv[z_of].astype(F32)
         lat[8 * z_of : 8 * z_of + 8, :] = jnp.concatenate([rows[0:8], rows[8:16]], axis=1)
     for index in range(12):
-        pl.when(unit_core(index) != core)(
+        pl.when(lax.rem(unit_quad(index), 2) != core)(
             lambda index=index: wait_in(wqkv.at[index], rs_w.at[index])
         )
     local[7].wait()
+    local[11].wait()
+    local[12].wait()
     wait_in(mixrecv.at[pl.ds(0, 15)], rs.at[6])
     for p in range(8):
         even, odd = mixrecv[2 * p].astype(F32), mixrecv[2 * p + 1].astype(F32)
@@ -316,6 +371,10 @@
     ]
     for copy in kv_copies:
         copy.start()
+    wait_in(selfo.at[pl.ds(0, 12), 0], rs.at[10])
+    forward_o = remote(selfo.at[:, core], selfo.at[:, core], ss.at[31], rs.at[7], sib)
+    forward_o.start()
+
     for other in (1, 2, 3):
         slot = lax.rem(quad + other, 4)
         wait_in(kvall.at[slot], rs_kv.at[slot])
@@ -376,15 +435,21 @@
     wait_out(ids_all.at[pl.ds(0, 15)], ss.at[0])
     wait_out(qbuf.at[0, pl.ds(0, 15)], ss.at[1])
     wait_out(strecv.at[pl.ds(0, 7)], ss.at[2])
-    for copy in own_up + forwards + kv_copies + [forward_q, swap, forward_o]:
+    for copy in own_up + forwards + kv_copies + along_x + along_y + [forward_q, swap, forward_o]:
         copy.wait_send()
     for i in range(3):
-        for x_of in range(2):
-            target, away, _ = unit_copies(i, x_of)
-            pl.when(target != me)(away.wait_send)
+        target, away, _ = unit_copies(i)
+        pl.when(target != me)(away.wait_send)
     for index in range(12):
-        pl.when(unit_core(index) == core)(lambda index=index: unit_forward(index).wait_send())
-    wait_out(selfo.at[pl.ds(0, 15), 0], ss.at[13])
+        pl.when(lax.rem(unit_quad(index), 2) == core)(
+            lambda index=index: unit_forward(index).wait_send()
+        )
+        pl.when(unit_quad(index) == quad)(lambda index=index: unit_across(index).wait_send())
+
+    @pl.when(carrier)
+    def _():
+        wait_out(selfo.at[pl.ds(0, 7), 0], ss.at[13])
+
     wait_out(mixrecv.at[pl.ds(0, 15)], ss.at[30])
     wait_out(mix2all.at[pl.ds(0, 7)], ss.at[35])
     wait_out(precv.at[pl.ds(0, 7)], ss.at[36])
@@ -396,14 +461,20 @@
 ):
     base, start, lanes = trig_tables()
     vmem = pl.BlockSpec(memory_space=pltpu.VMEM)
-    anywhere = pl.BlockSpec(memory_space=pl.ANY)
     dma = pltpu.SemaphoreType.DMA
     return pl.pallas_call(
         kernel,
         out_shape=jax.ShapeDtypeStruct((8, 1024), F32),
-        in_specs=[vmem] * 9 + [anywhere] * 7,
+        in_specs=[pl.BlockSpec(memory_space=pltpu.HBM)] * 16,
         out_specs=vmem,
         scratch_shapes=[
+            pltpu.VMEM((1, 1024), jnp.int32),
+            pltpu.VMEM((8, 1024), BF16),
+            pltpu.VMEM((1, 256), jnp.int32),
+            pltpu.VMEM((1, 1024), F32),
+            pltpu.VMEM((1, 1024), F32),
+            pltpu.VMEM((64, 128), F32),
+            pltpu.VMEM((8, 128), F32),
             pltpu.VMEM((1024, 1024), BF16),
             pltpu.VMEM((256, 1024), BF16),
             pltpu.VMEM((1024, 128), BF16),
@@ -419,7 +490,7 @@
             pltpu.VMEM((16, 1, 1024), jnp.int32),
             pltpu.VMEM((16, 512), BF16),
             pltpu.VMEM((8, 16, 512), BF16),
-            pltpu.VMEM((4, 32, 1024), BF16),
+            pltpu.VMEM((128, 1024), BF16),
             pltpu.VMEM((12, 32, 1024), BF16),
             pltpu.VMEM((16, 2, 32, 1024), BF16),
             pltpu.VMEM((256, 128), F32),
@@ -435,21 +506,21 @@
             pltpu.VMEM((8, 8, 1024), F32),
             pltpu.VMEM((8, 8, 1024), F32),
             pltpu.VMEM((8, 8, 1024), F32),
-            dma((8,)),
-            dma((37,)),
-            dma((10,)),
+            dma((17,)),
+            dma((57,)),
+            dma((12,)),
             dma((4,)),
             dma((4,)),
             dma((12,)),
             dma((4,)),
         ],
         compiler_params=pltpu.CompilerParams(
-            collective_id=0, has_side_effects=True, vmem_limit_bytes=48 << 20
+            collective_id=0, has_side_effects=True, vmem_limit_bytes=60 << 20
         ),
         name="ar_step",
     )(
         context_ids.reshape(1, -1), latent_states, limits.reshape(1, -1),
-        attn_gain.reshape(1, -1), mlp_gain.reshape(1, -1), self_qkv, self_o,
+        attn_gain.reshape(1, -1), mlp_gain.reshape(1, -1), self_qkv.T, self_o.T,
         jnp.asarray(start), jnp.asarray(lanes), jnp.asarray(base),
         embed_table, cross_q, cross_kv, cross_o, mlp_up, mlp_down,
     )

time: 95.1 us -> 68.1 us (0.72)
  Pallas kernels: 79.8 us -> 66 us
  local copies, waits for them, and re-layouts: 14.7 us -> 1.38 us
    pallas_call x1, Pallas kernels: 79.8 us -> 66 us  [on_device(): pl.pallas_call(kernel, out_shape=jax.ShapeDtypeStruct((8, 1024), F32), in...]
    unnamed x29 -> x1, local copies, waits for them, and re-layouts: 14.7 us -> 1.38 us
where the time goes in v2:
time: 68.1 us; the launch traced here: 67.3 us
  Pallas kernels  66 us (97%)
  local copies, waits for them, and re-layouts  1.38 us (2%)
    pallas_call x1, Pallas kernels, on_device(): pl.pallas_call(kernel, out_shape=jax.ShapeDtypeStruct((8, 1024), F32), in...  66 us
    unnamed x1, local copies, waits for them, and re-layouts  1.38 us

profile of v2, /device:TPU:16, one launch (start us, length us, event | category | flops | bytes accessed | tf_op | source)
XLA Modules:
  0.0 67.3 jit_solution(8726470137990890449)
XLA Ops:
  0.0 66.0 %ar_step.1 = f32[8,1024]{1,0:T(8,128)} custom-call(s32[1,1024]{1,0:T(1,128)} %bitcast.8, bf16[8,1024]{1,0:T(8,128)(2,1)} %states_hbm.1, s32[1,256]{1,0:T(1,128)} %bitcast.11, f32[1,1024]{1,0:T(1,128)} %bitcast.9, f32[1,1024]{1,0:T(1,128)} %bitcast.10, bf16[96,1024]{1,0:T(8,128)(2,1)} %bitcast.6, bf16[32,1024]{1,0:T(8,128)(2,1)} %bitcast.7, ...), custom_call_target="tpu_custom_call" | custom-call | tf_op jit(solution)/shard_map/ar_step/pallas_call | solution.py:465
  66.0 1.4 %copy.18 = f32[8,1024]{1,0:T(8,128)} copy(f32[8,1024]{1,0:T(8,128)} %ar_step.1) | data formatting | bytes 65536

commit v3 on v2

--- a/solution.py
+++ b/solution.py
@@ -55,7 +55,7 @@
     ids_ref, states_ref, limits_ref, attn_gain, mlp_gain, start_ref, lanes_ref,
     crossq, embed, ck, cv, base, crosso, updown_up, updown_dn,
     lim_nat, lim_perm, qsrc, qbuf, ids_all, stpack, strecv, wt, wqkv, selfo,
-    acc, peak, packs, comb, mixsrc, mixrecv, mixf, lat, kvall, mix2all, atts, part, precv,
+    keys_at, values_at, acc, peak, packs, comb, mixsrc, mixrecv, mixf, lat, kvall, mix2all, atts, part, precv, whole,
     loc, ss, rs, rs_up, rs_dn, rs_w, rs_kv,
 ):
     me = lax.axis_index("seq")
@@ -73,8 +73,9 @@
     carrier = lax.rem(z, 4) == y
     quad_x = quad + 2 - 4 * x
 
-    def same_core(i):
-        return lax.rem(chip + i, 16)
+    offsets = [(dz, dx) for dz in (4, 3, 5, 2, 6, 1, 7, 0) for dx in (1, 0) if dz or dx]
+    same_core = [2 * lax.rem(z + dz, 8) + lax.rem(x + dx, 2) for dz, dx in offsets]
+    ring = [lax.rem(me + 4 * dz, 32) for dz in (4, 3, 5, 2, 6, 1, 7)]
 
     def remote(src, dst, send, recv, seq, part_of=None):
         where = {"seq": seq} if part_of is None else {"dp": part_of, "seq": seq}
@@ -82,8 +83,9 @@
             src_ref=src, dst_ref=dst, send_sem=send, recv_sem=recv, device_id=where, device_id_type=MESH
         )
 
-    def over(count, body):
-        lax.fori_loop(1, count, lambda i, carry: (body(i), carry)[1], 0)
+    def over(targets, body):
+        for target in targets:
+            body(target)
 
     barrier = pltpu.get_barrier_semaphore()
 
@@ -91,11 +93,11 @@
         where = {"seq": seq} if part_of is None else {"dp": part_of, "seq": seq}
         pl.semaphore_signal(barrier, inc=1, device_id=where, device_id_type=MESH)
 
-    over(16, lambda i: greet(2 * same_core(i) + core))
+    over(same_core, lambda k: greet(2 * k + core))
     greet(sib)
     greet(diagonal)
     greet(across, dp_pair)
-    over(4, lambda i: greet(me, lax.rem(dp + 2 * i, 8)))
+    over((1, 2, 3), lambda i: greet(me, lax.rem(dp + 2 * i, 8)))
 
     columns = pl.multiple_of(128 * z, 128)
     local = [
@@ -156,26 +158,40 @@
 
     pl.semaphore_wait(barrier, 21)
 
-    def send_ids(i):
-        k = same_core(i)
+    def send_ids(k):
         remote(ids_ref, ids_all.at[chip], ss.at[0], rs.at[0], 2 * k + core).start()
+
+    def send_queries(k):
         remote(qsrc.at[k // 2], qbuf.at[core, x * 8 + z], ss.at[1], rs.at[1], 2 * k + core).start()
 
-    over(16, send_ids)
-
-    def ring(i):
-        return lax.rem(me + 4 * i, 32)
-
-    over(8, lambda i: remote(stpack, strecv.at[z], ss.at[2], rs.at[2], ring(i)).start())
+    over(same_core, send_ids)
+    over(same_core, send_queries)
+
+    over(ring, lambda seq: remote(stpack, strecv.at[z], ss.at[2], rs.at[2], seq).start())
     local[16].wait()
 
-    def send_selfo(i):
-        remote(wt.at[pl.ds(96, 32)], selfo.at[chip, core], ss.at[13], rs.at[3], ring(i)).start()
+    def send_selfo(seq):
+        remote(wt.at[pl.ds(96, 32)], selfo.at[chip, core], ss.at[13], rs.at[3], seq).start()
 
     @pl.when(carrier)
     def _():
         selfo[chip, core] = wt[96:128, :]
-        over(8, send_selfo)
+        over(ring, send_selfo)
+
+    local[15].wait()
+
+    def unit_copies(i):
+        unit = 3 * me + i
+        index = 4 * (unit // 32) + lax.rem(unit, 4)
+        target = 4 * (lax.rem(unit, 32) // 4) + quad
+        away = remote(wt.at[pl.ds(32 * i, 32)], wqkv.at[index], ss.at[7 + i], rs_w.at[index], target)
+        here = pltpu.make_async_copy(wt.at[pl.ds(32 * i, 32)], wqkv.at[index], rs_w.at[index])
+        return target, away, here
+
+    for i in range(3):
+        target, away, here = unit_copies(i)
+        pl.when(target != me)(away.start)
+        pl.when(target == me)(here.start)
 
     own_up = [
         remote(up_hbm, updown_up.at[quad], ss.at[3], rs_up.at[quad], sib),
@@ -203,34 +219,10 @@
         pltpu.make_async_copy(buf, buf, sem).wait()
 
     wait_in(ids_all.at[pl.ds(0, 15)], rs.at[0])
-    wait_in(qbuf.at[core, pl.ds(0, 15)], rs.at[1])
-    forward_q = remote(qbuf.at[core], qbuf.at[core], ss.at[14], rs.at[4], sib)
-    forward_q.start()
-    wait_in(qbuf.at[1 - core], rs.at[4])
-
-    local[15].wait()
-
-    def unit_copies(i):
-        unit = 3 * me + i
-        index = 4 * (unit // 32) + lax.rem(unit, 4)
-        target = 4 * (lax.rem(unit, 32) // 4) + quad
-        away = remote(wt.at[pl.ds(32 * i, 32)], wqkv.at[index], ss.at[7 + i], rs_w.at[index], target)
-        here = pltpu.make_async_copy(wt.at[pl.ds(32 * i, 32)], wqkv.at[index], rs_w.at[index])
-        return target, away, here
-
-    for i in range(3):
-        target, away, here = unit_copies(i)
-        pl.when(target != me)(away.start)
-        pl.when(target == me)(here.start)
-
-    lane256 = iota((256, 128), 1)
-    queries = jnp.where(lane256 // 64 == x, qbuf[...].reshape(256, 128), 0.0).astype(BF16)
-    acc[...] = jnp.zeros((256, 128), F32)
-    peak[...] = jnp.full((256, 128), LOW, F32)
-
-    def context_block(j, masked):
+    def key_block(j, slot):
         block = 2 * j + core
-        onehot = (iota((256, 1024), 0) == ids_all[j]).astype(F32).astype(BF16)
+        ids = jnp.broadcast_to(ids_all[j].astype(F32).astype(BF16), (256, 1024))
+        onehot = jnp.where(iota((256, 1024), 0).astype(F32).astype(BF16) == ids, 1.0, 0.0).astype(BF16)
         rows = dot(table, onehot)
         keys = rows[0:64] + rows[64:128]
         here = jnp.where(iota((64, 128), 1) == block, start_ref[...], 0.0)
@@ -240,23 +232,47 @@
         sin = sin_a * cos_b + cos_a * sin_b
         one, two = keys[0:32], keys[32:64]
         turned = jnp.concatenate([one * cos - two * sin, two * cos + one * sin], axis=0)
-        turned = turned.astype(BF16)
+        keys_at[slot] = turned.astype(BF16)
+        values_at[slot] = rows[128:192].astype(BF16)
+
+    for slot in range(4):
+        key_block(slot, slot)
+    wait_in(qbuf.at[core, pl.ds(0, 15)], rs.at[1])
+    forward_q = remote(qbuf.at[core], qbuf.at[core], ss.at[14], rs.at[4], sib)
+    forward_q.start()
+    wait_in(qbuf.at[1 - core], rs.at[4])
+    lane256 = iota((256, 128), 1)
+    queries = jnp.where(lane256 // 64 == x, qbuf[...].reshape(256, 128), 0.0).astype(BF16)
+    acc[...] = jnp.zeros((256, 128), F32)
+    peak[...] = jnp.full((256, 128), LOW, F32)
+
+    def context_block(j, slot, masked):
+        block = 2 * j + core
+        turned = keys_at[slot]
         scores = dot(queries, jnp.concatenate([turned, turned], axis=0))
         if masked:
             place = (block * 1024 + iota((1, 1024), 1)).astype(F32)
             scores = jnp.where(place < lim_perm[:, 0:1], scores, LOW)
         top = jnp.max(scores, axis=1, keepdims=True)
         weights = jnp.exp(scores - top).astype(BF16)
-        values = jnp.concatenate([rows[128:192].astype(BF16), jnp.ones((64, 1024), BF16)], axis=0)
+        values = jnp.concatenate([values_at[slot], jnp.ones((64, 1024), BF16)], axis=0)
         terms = dot_nt(weights, values)
         old = peak[...]
         new = jnp.maximum(old, top)
         acc[...] = acc[...] * jnp.exp(old - new) + terms * jnp.exp(top - new)
         peak[...] = new
 
-    lax.fori_loop(0, 8, lambda j, carry: (context_block(j, False), carry)[1], 0, unroll=4)
-
-    lax.fori_loop(8, 12, lambda j, carry: (context_block(j, True), carry)[1], 0, unroll=4)
+    @pl.loop(0, 8, step=4)
+    def _(start):
+        for slot in range(4):
+            context_block(start + slot, slot, False)
+            key_block(start + slot + 4, slot)
+
+    @pl.loop(8, 12, step=4)
+    def _(start):
+        for slot in range(4):
+            context_block(start + slot, slot, True)
+            key_block(start + slot + 4, slot)
 
     @pl.when(carrier)
     def _():
@@ -291,7 +307,10 @@
     for index in range(12):
         pl.when(unit_quad(index) == quad)(lambda index=index: turn_unit(index))
 
-    lax.fori_loop(12, 16, lambda j, carry: (context_block(j, True), carry)[1], 0, unroll=4)
+    @pl.loop(12, 16, step=4)
+    def _(start):
+        for slot in range(4):
+            context_block(start + slot, slot, True)
 
     wait_in(selfo.at[pl.ds(0, 2), 0], rs.at[11])
     along_y = []
@@ -336,11 +355,10 @@
         mixsrc[x_of] = jnp.where(lane32 < 64, low, pltpu.roll(high, 64, 1)).astype(BF16)
     mixrecv[chip] = mixsrc[x]
 
-    def send_mix(i):
-        k = same_core(i)
+    def send_mix(k):
         remote(mixsrc.at[lax.rem(k, 2)], mixrecv.at[chip], ss.at[30], rs.at[6], 2 * k + core).start()
 
-    over(16, send_mix)
+    over(same_core, send_mix)
 
     wait_in(strecv.at[pl.ds(0, 7)], rs.at[2])
     for z_of in range(8):
@@ -396,7 +414,7 @@
         fine = (weights - coarse.astype(F32)).astype(BF16)
         heads.append((dot(coarse, values) + dot(fine, values)) / total)
     mix2all[z] = jnp.where(lane64 < 64, heads[0], heads[1]).astype(BF16)
-    over(8, lambda i: remote(mix2all.at[z], mix2all.at[z], ss.at[35], rs.at[8], ring(i)).start())
+    over(ring, lambda seq: remote(mix2all.at[z], mix2all.at[z], ss.at[35], rs.at[8], seq).start())
     wait_in(selfo.at[:, 1 - core], rs.at[7])
     wait_in(mix2all.at[pl.ds(0, 7)], rs.at[8])
     mix2 = jnp.concatenate([mix2all[k] for k in range(8)], axis=1)
@@ -414,20 +432,23 @@
         ups = jnp.concatenate([updown_up[2 * half], updown_up[2 * half + 1]], axis=1)
         hidden.append(jax.nn.gelu(dot(normed, ups), approximate=True).astype(BF16))
     hidden = jnp.concatenate(hidden, axis=1)
-    part[...] = dot(hidden, updown_dn[...].reshape(512, 1024)).reshape(8, 8, 1024)
-    precv[z] = part[z]
-
-    def send_part(i):
-        seq = ring(i)
+    terms = dot(hidden, updown_dn[...].reshape(512, 1024))
+    for k in range(8):
+        rows = terms[8 * k : 8 * k + 8]
+        part[k] = jnp.concatenate([rows[:, :512], rows[:, 512:]], axis=0).astype(BF16)
+
+    def send_part(seq):
         remote(part.at[seq // 4], precv.at[z], ss.at[36], rs.at[9], seq).start()
 
-    over(8, send_part)
+    over(ring, send_part)
+    whole[...] = terms.reshape(8, 8, 1024)
+    own = whole[z]
+    precv[z] = jnp.zeros((16, 512), BF16)
     wait_in(precv.at[pl.ds(0, 7)], rs.at[9])
-    total = atts[z]
-    summed = precv[0]
+    summed = precv[0].astype(F32)
     for k in range(1, 8):
-        summed = summed + precv[k]
-    out_ref[...] = total + summed
+        summed = summed + precv[k].astype(F32)
+    out_ref[...] = atts[z] + (own + jnp.concatenate([summed[:8], summed[8:]], axis=1))
 
     def wait_out(buf, sem):
         pltpu.make_async_copy(buf, buf, sem).wait()
@@ -493,6 +514,8 @@
             pltpu.VMEM((128, 1024), BF16),
             pltpu.VMEM((12, 32, 1024), BF16),
             pltpu.VMEM((16, 2, 32, 1024), BF16),
+            pltpu.VMEM((4, 64, 1024), BF16),
+            pltpu.VMEM((4, 64, 1024), BF16),
             pltpu.VMEM((256, 128), F32),
             pltpu.VMEM((256, 128), F32),
             pltpu.VMEM((2, 128, 128), F32),
@@ -504,7 +527,8 @@
             pltpu.VMEM((4, 64, 256), BF16),
             pltpu.VMEM((8, 64, 128), BF16),
             pltpu.VMEM((8, 8, 1024), F32),
-            pltpu.VMEM((8, 8, 1024), F32),
+            pltpu.VMEM((8, 16, 512), BF16),
+            pltpu.VMEM((8, 16, 512), BF16),
             pltpu.VMEM((8, 8, 1024), F32),
             dma((17,)),
             dma((57,)),

time: 68.1 us -> 63.1 us (0.927)
  Pallas kernels: 66 us -> 61.6 us
    pallas_call x1, Pallas kernels: 66 us -> 61.6 us  [on_device(): pl.pallas_call(kernel, out_shape=jax.ShapeDtypeStruct((8, 1024), F32), in...]
where the time goes in v3:
time: 63.1 us; the launch traced here: 63 us
  Pallas kernels  61.6 us (98%)
  local copies, waits for them, and re-layouts  1.38 us (2%)
    pallas_call x1, Pallas kernels, on_device(): pl.pallas_call(kernel, out_shape=jax.ShapeDtypeStruct((8, 1024), F32), in...  61.6 us
    unnamed x1, local copies, waits for them, and re-layouts  1.38 us

profile of v3, /device:TPU:16, one launch (start us, length us, event | category | flops | bytes accessed | tf_op | source)
XLA Modules:
  0.0 63.0 jit_solution(8106214146329591159)
XLA Ops:
  0.0 61.6 %ar_step.1 = f32[8,1024]{1,0:T(8,128)} custom-call(s32[1,1024]{1,0:T(1,128)} %bitcast.8, bf16[8,1024]{1,0:T(8,128)(2,1)} %states_hbm.1, s32[1,256]{1,0:T(1,128)} %bitcast.11, f32[1,1024]{1,0:T(1,128)} %bitcast.9, f32[1,1024]{1,0:T(1,128)} %bitcast.10, bf16[96,1024]{1,0:T(8,128)(2,1)} %bitcast.6, bf16[32,1024]{1,0:T(8,128)(2,1)} %bitcast.7, ...), custom_call_target="tpu_custom_call" | custom-call | tf_op jit(solution)/shard_map/ar_step/pallas_call | solution.py:486
  61.6 1.4 %copy.18 = f32[8,1024]{1,0:T(8,128)} copy(f32[8,1024]{1,0:T(8,128)} %ar_step.1) | data formatting | bytes 65536

commit v4 on v3

--- a/solution.py
+++ b/solution.py
@@ -336,13 +336,6 @@
     for copy in forwards:
         copy.start()
 
-    def pass_unit(index):
-        wait_in(wqkv.at[index], rs_w.at[index])
-        unit_forward(index).start()
-
-    for index in range(12):
-        pl.when(unit_quad(index) == quad_x)(lambda index=index: pass_unit(index))
-
     wait_in(comb, rs.at[5])
     mine, theirs = packs[core], comb[...]
     peak_a, peak_b = mine[:, 127:128], theirs[:, 127:128]
@@ -359,6 +352,14 @@
         remote(mixsrc.at[lax.rem(k, 2)], mixrecv.at[chip], ss.at[30], rs.at[6], 2 * k + core).start()
 
     over(same_core, send_mix)
+
+    def pass_unit(index):
+        wait_in(wqkv.at[index], rs_w.at[index])
+        unit_forward(index).start()
+
+    for index in range(12):
+        pl.when(unit_quad(index) == quad_x)(lambda index=index: pass_unit(index))
+
 
     wait_in(strecv.at[pl.ds(0, 7)], rs.at[2])
     for z_of in range(8):

time: 63.1 us -> 61.6 us (0.976); the launches traced: 63 us -> 60.5 us
  Pallas kernels: 61.6 us -> 59.1 us
    pallas_call x1, Pallas kernels: 61.6 us -> 59.1 us  [on_device(): pl.pallas_call(kernel, out_shape=jax.ShapeDtypeStruct((8, 1024), F32), in...]
where the time goes in v4:
time: 61.6 us; the launch traced here: 60.5 us
  Pallas kernels  59.1 us (96%)
  local copies, waits for them, and re-layouts  1.38 us (2%)
    pallas_call x1, Pallas kernels, on_device(): pl.pallas_call(kernel, out_shape=jax.ShapeDtypeStruct((8, 1024), F32), in...  59.1 us
    unnamed x1, local copies, waits for them, and re-layouts  1.38 us

profile of v4, /device:TPU:16, one launch (start us, length us, event | category | flops | bytes accessed | tf_op | source)
XLA Modules:
  0.0 60.5 jit_solution(9878510352273604738)
XLA Ops:
  0.0 59.1 %ar_step.1 = f32[8,1024]{1,0:T(8,128)} custom-call(s32[1,1024]{1,0:T(1,128)} %bitcast.8, bf16[8,1024]{1,0:T(8,128)(2,1)} %states_hbm.1, s32[1,256]{1,0:T(1,128)} %bitcast.11, f32[1,1024]{1,0:T(1,128)} %bitcast.9, f32[1,1024]{1,0:T(1,128)} %bitcast.10, bf16[96,1024]{1,0:T(8,128)(2,1)} %bitcast.6, bf16[32,1024]{1,0:T(8,128)(2,1)} %bitcast.7, ...), custom_call_target="tpu_custom_call" | custom-call | tf_op jit(solution)/shard_map/ar_step/pallas_call | solution.py:487
  59.1 1.4 %copy.18 = f32[8,1024]{1,0:T(8,128)} copy(f32[8,1024]{1,0:T(8,128)} %ar_step.1) | data formatting | bytes 65536
